TPU v7x, 128 devices: a whole 4x4x4 slice. The times are simulated.
128 devices in a mesh: band: 32 (over z, y, x_hi), pair: 4 (over x_lo, core).
Axes of the slice: x: 4 (x_hi: 2, x_lo: 2; x = x_hi * 2 + x_lo), y: 4, z: 4, core: 2. Of those that a mesh axis runs over, the one named last changes fastest.
Arguments:
- orbitals: float32 [32, 64, 4096], P('band'), may hold values from -3 to 3
- pair_keep: int32 [32, 32], replicated, may hold values from 0 to 1, as said below
Outputs:
- exchange: float32 [32, 64, 4096], P('band', 'pair')
Inputs may be any that keep to these rules, and one draw needn't show every extreme that they name: pair_keep is symmetric with ones on its diagonal; orbital i belongs to block i.
All inputs are finite; a program needn't handle non-finite values.
Results may differ from a plain program's by a relative error of at most 0.00018.
Values sent between devices are 32-bit elements; how exact they have to be, the bound alone decides.
A program may use at most 128 MiB of HBM per device.

v0:
```python
import math

import jax
import jax.numpy as jnp
from jax import lax
from jax.sharding import PartitionSpec as P

NX = 64
NY = 64
NZ = 64


CELL_LENGTH = 46.92
SCREEN_OMEGA = 0.11
HIGHEST_PRECISION = lax.Precision.HIGHEST


def shifted(shard, axis, by):
    length = lax.axis_size(axis)
    return lax.ppermute(shard, axis, [(i, (i + by) % length) for i in range(length)])


def cas_table(length):
    counter = jnp.arange(length, dtype=jnp.int32)
    angles = (counter[:, None] * counter[None, :] % length).astype(jnp.float32) * (
        2.0 * math.pi / length
    )
    return jnp.cos(angles) + jnp.sin(angles)


def wave_numbers(length):
    counter = jnp.arange(length, dtype=jnp.int32)
    return jnp.minimum(counter, length - counter).astype(jnp.float32) * (
        2.0 * math.pi / CELL_LENGTH
    )


def screened_kernel():
    wave_x = wave_numbers(NX)
    wave_y = wave_numbers(NY)
    wave_z = wave_numbers(NZ)
    square = wave_x[:, None, None] ** 2 + wave_y[None, :, None] ** 2 + wave_z[None, None, :] ** 2
    guarded = jnp.where(square > 0.0, square, 1.0)
    screened = 4.0 * math.pi / guarded * -jnp.expm1(-guarded / (4.0 * SCREEN_OMEGA * SCREEN_OMEGA))
    return jnp.where(square > 0.0, screened, 0.0)


def convolve(density, tables):
    table_x, table_y, table_z, kernel = tables
    pairs_now = density.shape[0]
    cube_view = density.reshape(pairs_now, NX, NY, NZ)
    for cas_matrix in (table_x, table_y, table_z):
        cube_view = jnp.einsum("ka,qabc->qbck", cas_matrix, cube_view, precision=HIGHEST_PRECISION)
    cube_view = cube_view * kernel
    for cas_matrix in (table_x, table_y, table_z):
        cube_view = jnp.einsum("ka,qabc->qbck", cas_matrix, cube_view, precision=HIGHEST_PRECISION)
    return cube_view.reshape(pairs_now, NX, NY * NZ)


def visit_terms(own_block, partner_block, weight_own, weight_partner, tables):
    zero_block = jnp.zeros_like(own_block)

    def row_step(row_index, running):
        own_acc, partner_acc = running
        potential = convolve(own_block * partner_block, tables)
        own_weight = weight_own[0][:, None, None]
        partner_weight = weight_partner[0][:, None, None]
        own_term = jnp.sum(own_weight * potential * partner_block, axis=0, keepdims=True)
        updated = own_acc + own_term
        own_acc = updated
        partner_acc = partner_acc + partner_weight * potential * own_block
        return (own_acc, partner_acc)

    def full_work(operand):
        return lax.fori_loop(0, own_block.shape[0], row_step, (zero_block, zero_block))

    def no_work(operand):
        return (zero_block, zero_block)

    has_work = jnp.any(weight_own > 0.0) | jnp.any(weight_partner > 0.0)
    return lax.cond(has_work, full_work, no_work, 0)


def cycle_move(piece, offset):
    return shifted(piece, "band", offset)


def body(orbitals, pair_keep):
    per_band = orbitals.shape[0]
    band_count = lax.axis_size("band")
    row_count = lax.axis_size("pair")
    half_cycle = band_count // 2
    visits = half_cycle // row_count
    band_at = lax.axis_index("band")
    row_at = lax.axis_index("pair")
    tables = (
        cas_table(NX),
        cas_table(NY),
        cas_table(NZ),
        screened_kernel() * (-1.0 / (NX * NY * NZ)),
    )
    stride = 1
    keep_float = pair_keep.astype(jnp.float32)
    home_row = band_at * per_band
    self_keep = lax.dynamic_slice(keep_float, (home_row, home_row), (per_band, per_band))
    orbital_ids = jnp.arange(per_band, dtype=jnp.int32)
    assigned = (orbital_ids % row_count == row_at).astype(jnp.float32)[:, None]
    not_below = (orbital_ids[None, :] >= orbital_ids[:, None]).astype(jnp.float32)
    strictly_above = (orbital_ids[None, :] > orbital_ids[:, None]).astype(jnp.float32)
    own_acc, cross_acc = visit_terms(
        orbitals,
        orbitals,
        self_keep * not_below * assigned,
        self_keep * strictly_above * assigned,
        tables,
    )
    own_part = own_acc + cross_acc
    slab_rows = orbitals.shape[1] // row_count
    own_slab = lax.dynamic_slice_in_dim(orbitals, row_at * slab_rows, slab_rows, 1)
    pieces = jnp.stack(
        [cycle_move(own_slab, -(1 + turn_index * visits)) for turn_index in range(row_count)]
    )
    visitor = lax.all_to_all(pieces, "pair", split_axis=0, concat_axis=2, tiled=True)[0]
    returned = jnp.zeros_like(orbitals)
    for step_index in range(visits):
        if step_index > 0:
            visitor = shifted(visitor, "band", -stride)
        shift_now = 1 + row_at * visits + step_index * stride
        partner = (band_at + shift_now) % band_count
        block_keep = lax.dynamic_slice(
            keep_float, (home_row, partner * per_band), (per_band, per_band)
        )
        allowed = ((shift_now < half_cycle) | (band_at < half_cycle)).astype(jnp.float32)
        weights = block_keep * allowed
        own_acc, partner_acc = visit_terms(orbitals, visitor, weights, weights, tables)
        own_part = own_part + own_acc
        if step_index > 0:
            partner_acc = shifted(partner_acc, "band", step_index * stride)
        returned = returned + partner_acc
    own_slabs, return_slabs = (
        lax.all_to_all(own_part[None], "pair", split_axis=2, concat_axis=0, tiled=True),
        lax.all_to_all(returned[None], "pair", split_axis=2, concat_axis=0, tiled=True),
    )
    summed = jnp.sum(own_slabs, axis=0)
    for turn_index in range(row_count):
        summed = summed + cycle_move(return_slabs[turn_index], 1 + turn_index * visits)
    return summed


def solution(mesh):
    return jax.shard_map(
        body,
        mesh=mesh,
        in_specs=(P("band", None, None), P()),
        out_specs=P("band", "pair", None),
        check_vma=False,
    )
```

profile of v0, /device:TPU:32, one launch (start us, length us, event | category | flops | bytes accessed | tf_op | source)
XLA Modules:
  0.0 438.4 jit_solution(1514815546044360862)
XLA Ops:
  1.0 6.5 %collective-permute-start.3 = (f32[1,16,4096]{2,1,0:T(8,128)S(1)}, f32[1,16,4096]{2,1,0:T(8,128)S(1)}, u32[]{:S(2)}, u32[]{:S(2)}) collective-permute-start(f32[1,16,4096]{2,1,0:T(8,128)S(1)} %constant_dynamic-slice_fusion), channel_id=1, source_target_pairs={{0,76},{4,80},{8,84},{12,88},{16,92},{20,96},{24,100},{28,104},{32... | collective-permute-start | bytes 786440 | tf_op jit(solution)/shard_map/ppermute | solution.py:20
  21.1 7.2 %collective-permute-done.1 = f32[1,16,4096]{2,1,0:T(8,128)S(1)} collective-permute-done((f32[1,16,4096]{2,1,0:T(8,128)S(1)}, f32[1,16,4096]{2,1,0:T(8,128)S(1)}, u32[]{:S(2)}, u32[]{:S(2)}) %collective-permute-start.1) | collective-permute-done | bytes 262176 | tf_op jit(solution)/shard_map/ppermute | solution.py:20
  32.6 18.0 %all_to_all.33 = f32[4,1,16,4096]{3,2,1,0:T(8,128)S(1)} all-to-all(f32[4,1,16,4096]{3,2,1,0:T(8,128)S(1)} %pad_maximum_fusion), channel_id=1, replica_groups=mesh['band'=32,'pair'=4] {'pair'}, dimensions={0} | all-to-all | bytes 2097152 | tf_op jit(solution)/shard_map/all_to_all | solution.py:123
  55.7 22.1 %collective-permute-done.4 = f32[1,64,4096]{2,1,0:T(8,128)S(1)} collective-permute-done((f32[1,64,4096]{2,1,0:T(8,128)S(1)}, f32[1,64,4096]{2,1,0:T(8,128)S(1)}, u32[]{:S(2)}, u32[]{:S(2)}) %collective-permute-start.4) | collective-permute-done | bytes 1048608 | tf_op jit(solution)/shard_map/ppermute | solution.py:20
  78.8 7.0 %collective-permute-start.5 = (f32[1,64,4096]{2,1,0:T(8,128)S(1)}, f32[1,64,4096]{2,1,0:T(8,128)}, u32[]{:S(2)}, u32[]{:S(2)}) collective-permute-start(f32[1,64,4096]{2,1,0:T(8,128)S(1)} %collective-permute-done.4), channel_id=1, source_target_pairs={{0,124},{4,0},{8,4},{12,8},{16,12},{20,16},{24,20},{28,24},{32,28}... | collective-permute-start | bytes 3145736 | tf_op jit(solution)/shard_map/ppermute | solution.py:20
  85.8 21.1 %collective-permute-done.5 = f32[1,64,4096]{2,1,0:T(8,128)} collective-permute-done((f32[1,64,4096]{2,1,0:T(8,128)S(1)}, f32[1,64,4096]{2,1,0:T(8,128)}, u32[]{:S(2)}, u32[]{:S(2)}) %collective-permute-start.5) | collective-permute-done | bytes 1048608 | tf_op jit(solution)/shard_map/ppermute | solution.py:20
  106.9 7.1 %collective-permute-start.6 = (f32[1,64,4096]{2,1,0:T(8,128)}, f32[1,64,4096]{2,1,0:T(8,128)}, u32[]{:S(2)}, u32[]{:S(2)}) collective-permute-start(f32[1,64,4096]{2,1,0:T(8,128)} %collective-permute-done.5), channel_id=1, source_target_pairs={{0,124},{4,0},{8,4},{12,8},{16,12},{20,16},{24,20},{28,24},{32,28}... | collective-permute-start | bytes 3145736 | tf_op jit(solution)/shard_map/ppermute | solution.py:20
  118.2 46.7 %conditional.7 = (f32[1,64,4096]{2,1,0:T(8,128)}, f32[1,64,4096]{2,0,1:T(1,128)}) conditional(s32[]{:T(128)} %bitcast.51, () %tuple.59, (f32[1,1]{1,0:T(1,128)}, f32[1,64,4096]{2,1,0:T(8,128)S(1)}, f32[1,64,4096]{2,1,0:T(8,128)S(1)}, f32[64,64]{1,0:T(8,128)S(1)}, f32[64,64]{1,0:T(8,128)S(1)}, /*index=5*/f32[64,64]{1,0:T(8,128)S(1)}, ...), branch_computations={%region_4.5_spmd, %region_5.6_spmd} | conditional | flops 1209270272 | bytes 34701360 | solution.py:81
  136.0 6.1 %fusion.17 = f32[64,64,64]{2,1,0:T(8,128)} fusion(f32[64,64,64]{2,1,0:T(8,128)S(1)} %fusion.23, f32[64,64]{1,0:T(8,128)S(1)} %get-tuple-element.250), kind=kOutput, calls=%fused_computation.16 | convolution fusion | flops 201326592 | bytes 2113536 | tf_op jit(solution)/shard_map/cond/branch_1_fun/while/body/eval_jaxpr/ka,qabc->qbck/dot_general | solution.py:56
  146.2 7.7 %fusion.27 = f32[64,64,64]{0,2,1:T(8,128)S(1)} fusion(f32[64,64,64]{0,1,2:T(8,128)} %copy.30, f32[64,64]{1,0:T(8,128)S(1)} %get-tuple-element.250), kind=kOutput, calls=%fused_computation.25 | convolution fusion | flops 201326592 | bytes 2113536 | tf_op jit(solution)/shard_map/cond/branch_1_fun/while/body/eval_jaxpr/ka,qabc->qbck/dot_general | solution.py:56
  168.2 46.7 %conditional.8 = (f32[1,64,4096]{2,1,0:T(8,128)}, f32[1,64,4096]{2,0,1:T(1,128)}) conditional(s32[]{:T(128)} %bitcast.53, () %tuple.61, (f32[1,1]{1,0:T(1,128)}, f32[1,64,4096]{2,1,0:T(8,128)S(1)}, f32[1,64,4096]{2,1,0:T(8,128)}, f32[64,64]{1,0:T(8,128)S(1)}, f32[64,64]{1,0:T(8,128)S(1)}, /*index=5*/f32[64,64]{1,0:T(8,128)S(1)}, ...), branch_computations={%region_6.7_spmd, %region_7.8_spmd} | conditional | flops 1209270272 | bytes 30507028 | solution.py:81
  196.2 7.7 %fusion.44 = f32[64,64,64]{0,2,1:T(8,128)S(1)} fusion(f32[64,64,64]{0,1,2:T(8,128)} %copy.35, f32[64,64]{1,0:T(8,128)S(1)} %get-tuple-element.279), kind=kOutput, calls=%fused_computation.41 | convolution fusion | flops 201326592 | bytes 2113536 | tf_op jit(solution)/shard_map/cond/branch_1_fun/while/body/eval_jaxpr/ka,qabc->qbck/dot_general | solution.py:56
  218.2 46.6 %conditional.9 = (f32[1,64,4096]{2,1,0:T(8,128)}, f32[1,64,4096]{2,0,1:T(1,128)}) conditional(s32[]{:T(128)} %bitcast.55, () %tuple.63, (f32[1,1]{1,0:T(1,128)}, f32[1,64,4096]{2,1,0:T(8,128)S(1)}, f32[1,64,4096]{2,1,0:T(8,128)}, f32[64,64]{1,0:T(8,128)S(1)}, f32[64,64]{1,0:T(8,128)S(1)}, /*index=5*/f32[64,64]{1,0:T(8,128)S(1)}, ...), branch_computations={%region_8.9_spmd, %region_9.10_spmd} | conditional | flops 1209270272 | bytes 30507028 | solution.py:81
  246.1 7.7 %fusion.61 = f32[64,64,64]{0,2,1:T(8,128)S(1)} fusion(f32[64,64,64]{0,1,2:T(8,128)} %copy.40, f32[64,64]{1,0:T(8,128)S(1)} %get-tuple-element.289), kind=kOutput, calls=%fused_computation.57 | convolution fusion | flops 201326592 | bytes 2113536 | tf_op jit(solution)/shard_map/cond/branch_1_fun/while/body/eval_jaxpr/ka,qabc->qbck/dot_general | solution.py:56
  269.9 48.2 %conditional.5 = (f32[1,64,4096]{2,0,1:T(1,128)}) conditional(s32[]{:T(128)} %bitcast.42, () %tuple.55, (f32[1,1]{1,0:T(1,128)}, f32[1,64,4096]{2,1,0:T(8,128)S(1)}, f32[64,64]{1,0:T(8,128)S(1)}, f32[64,64]{1,0:T(8,128)S(1)}, f32[64,64]{1,0:T(8,128)S(1)}, /*index=5*/f32[64,64,64]{2,1,0:T(8,128)S(1)}, f32[64,64]{1,0:T(8,128)S(1)}, ...), branch_computations={%region_0.1_spmd.clone, %region_1.2_spmd.clone} | conditional | flops 1209794560 | bytes 34701328 | solution.py:81
  296.6 7.7 %fusion.79 = f32[64,64,64]{0,2,1:T(8,128)S(1)} fusion(f32[64,64,64]{0,1,2:T(8,128)} %copy.65, f32[64,64]{1,0:T(8,128)S(1)} %get-tuple-element.326), kind=kOutput, calls=%fused_computation.76 | convolution fusion | flops 201326592 | bytes 2113536 | tf_op jit(solution)/shard_map/cond/branch_1_fun/while/body/eval_jaxpr/ka,qabc->qbck/dot_general | solution.py:56
  318.1 42.1 %conditional.6 = (f32[1,64,4096]{2,0,1:T(1,128)}, f32[1,64,4096]{2,0,1:T(1,128)S(1)}) conditional(s32[]{:T(128)} %bitcast.44, () %tuple.57, (f32[1,1]{1,0:T(1,128)}, f32[1,64,4096]{2,1,0:T(8,128)S(1)}, f32[1,64,4096]{2,1,0:T(8,128)}, f32[64,64]{1,0:T(8,128)S(1)}, f32[64,64]{1,0:T(8,128)S(1)}, /*index=5*/f32[64,64]{1,0:T(8,128)S(1)}, ...), branch_computations={%region_2.3_spmd, %region_3.4_spmd} | conditional | flops 1209270272 | bytes 36798512 | solution.py:81
  343.4 7.7 %fusion.10 = f32[64,64,64]{0,2,1:T(8,128)S(1)} fusion(f32[64,64,64]{0,1,2:T(8,128)} %copy.25, f32[64,64]{1,0:T(8,128)S(1)} %get-tuple-element.230), kind=kOutput, calls=%fused_computation.9 | convolution fusion | flops 201326592 | bytes 2113536 | tf_op jit(solution)/shard_map/cond/branch_1_fun/while/body/eval_jaxpr/ka,qabc->qbck/dot_general | solution.py:56
  360.1 6.6 %add_bitcast_fusion = f32[1,1,64,4096]{3,1,0,2:T(1,128)} fusion(f32[1,64,4096]{2,0,1:T(1,128)} %collective-permute-done.9, f32[1,64,4096]{2,0,1:T(1,128)} %collective-permute-done.8, f32[1,64,4096]{2,0,1:T(1,128)S(1)} %get-tuple-element.313, f32[1,64,4096]{2,0,1:T(1,128)} %collective-permute-done.7), kind=kLoop, calls=%fused_computation.94 | loop fusion | flops 786432 | bytes 5242880 | tf_op jit(solution)/shard_map/broadcast_in_dim | solution.py:142
  370.2 6.7 %add_bitcast_fusion.1 = f32[1,1,64,4096]{3,1,0,2:T(1,128)} fusion(f32[1,64,4096]{2,0,1:T(1,128)} %get-tuple-element.316, f32[1,64,4096]{2,0,1:T(1,128)} %get-tuple-element.315, f32[1,64,4096]{2,0,1:T(1,128)} %get-tuple-element.314, f32[1,64,4096]{2,0,1:T(1,128)} %get-tuple-element.311, f32[1,64,4096]{2,0,1:T(1,128)} %get-tuple-element.312), kind=kLoop, calls=%fused_computation.95 | loop fusion | flops 1048576 | bytes 6291456 | tf_op jit(solution)/shard_map/broadcast_in_dim | solution.py:141
  377.0 7.7 %all-to-all-done.2 = f32[1,1,64,4096]{3,1,0,2:T(1,128)S(1)} async-done(((f32[1,1,64,4096]{3,1,0,2:T(1,128)}), f32[1,1,64,4096]{3,1,0,2:T(1,128)S(1)}, u32[]{:S(2)}, u32[]{:S(2)}) %all-to-all-start.2) | async-done | bytes 1048608 | tf_op jit(solution)/shard_map/all_to_all | solution.py:142
  388.2 11.1 %collective-permute-start.13 = (f32[1,16,4096]{2,0,1:T(1,128)S(1)}, f32[1,16,4096]{2,0,1:T(1,128)S(1)}, u32[]{:S(2)}, u32[]{:S(2)}) collective-permute-start(f32[1,16,4096]{2,0,1:T(1,128)S(1)} %slice_bitcast_fusion), channel_id=1, source_target_pairs={{0,52},{4,56},{8,60},{12,64},{16,68},{20,72},{24,76},{28,80},{32,8... | collective-permute-start | bytes 786440 | tf_op jit(solution)/shard_map/ppermute | solution.py:20
  406.3 9.2 %collective-permute-done.12 = f32[1,16,4096]{2,0,1:T(1,128)S(1)} collective-permute-done((f32[1,16,4096]{2,0,1:T(1,128)}, f32[1,16,4096]{2,0,1:T(1,128)S(1)}, u32[]{:S(2)}, u32[]{:S(2)}) %collective-permute-start.12) | collective-permute-done | bytes 262176 | tf_op jit(solution)/shard_map/ppermute | solution.py:20
  415.5 15.4 %collective-permute-done.11 = f32[1,16,4096]{2,0,1:T(1,128)S(1)} collective-permute-done((f32[1,16,4096]{2,0,1:T(1,128)}, f32[1,16,4096]{2,0,1:T(1,128)S(1)}, u32[]{:S(2)}, u32[]{:S(2)}) %collective-permute-start.11) | collective-permute-done | bytes 262176 | tf_op jit(solution)/shard_map/ppermute | solution.py:20
  (110 shorter events, 242.7 us)
Async XLA Ops:
  1.0 15.8 %collective-permute-start.3 = (f32[1,16,4096]{2,1,0:T(8,128)S(1)}, f32[1,16,4096]{2,1,0:T(8,128)S(1)}, u32[]{:S(2)}, u32[]{:S(2)}) collective-permute-start(f32[1,16,4096]{2,1,0:T(8,128)S(1)} %constant_dynamic-slice_fusion), channel_id=1, source_target_pairs={{0,76},{4,80},{8,84},{12,88},{16,92},{20,96},{24,100},{28,104},{32... | collective-permute-start | bytes 786440 | tf_op jit(solution)/shard_map/ppermute | solution.py:20
  7.5 13.6 %collective-permute-start.2 = (f32[1,16,4096]{2,1,0:T(8,128)S(1)}, f32[1,16,4096]{2,1,0:T(8,128)S(1)}, u32[]{:S(2)}, u32[]{:S(2)}) collective-permute-start(f32[1,16,4096]{2,1,0:T(8,128)S(1)} %constant_dynamic-slice_fusion), channel_id=1, source_target_pairs={{0,92},{4,96},{8,100},{12,104},{16,108},{20,112},{24,116},{28,120}... | collective-permute-start | bytes 786440 | tf_op jit(solution)/shard_map/ppermute | solution.py:20
  9.9 18.3 %collective-permute-start.1 = (f32[1,16,4096]{2,1,0:T(8,128)S(1)}, f32[1,16,4096]{2,1,0:T(8,128)S(1)}, u32[]{:S(2)}, u32[]{:S(2)}) collective-permute-start(f32[1,16,4096]{2,1,0:T(8,128)S(1)} %constant_dynamic-slice_fusion), channel_id=1, source_target_pairs={{0,108},{4,112},{8,116},{12,120},{16,124},{20,0},{24,4},{28,8},{32... | collective-permute-start | bytes 786440 | tf_op jit(solution)/shard_map/ppermute | solution.py:20
  12.6 19.9 %collective-permute-start = (f32[1,16,4096]{2,1,0:T(8,128)S(1)}, f32[1,16,4096]{2,1,0:T(8,128)S(1)}, u32[]{:S(2)}, u32[]{:S(2)}) collective-permute-start(f32[1,16,4096]{2,1,0:T(8,128)S(1)} %constant_dynamic-slice_fusion), channel_id=1, source_target_pairs={{0,124},{4,0},{8,4},{12,8},{16,12},{20,16},{24,20},{28,24},{32,28}... | collective-permute-start | bytes 786440 | tf_op jit(solution)/shard_map/ppermute | solution.py:20
  32.5 81.5 %copy-start.6 = (s32[32,32]{1,0:T(8,128)S(1)}, s32[32,32]{1,0:T(8,128)}, u32[]{:S(2)}) copy-start(s32[32,32]{1,0:T(8,128)} %param.13) | copy-start | bytes 12292
  32.6 85.6 %copy-start = (f32[1,64,4096]{2,1,0:T(8,128)S(1)}, f32[1,64,4096]{2,1,0:T(8,128)}, u32[]{:S(2)}) copy-start(f32[1,64,4096]{2,1,0:T(8,128)} %param.12) | copy-start | bytes 3145732
  50.6 1.0 copy-start.1
  51.6 26.2 %collective-permute-start.4 = (f32[1,64,4096]{2,1,0:T(8,128)S(1)}, f32[1,64,4096]{2,1,0:T(8,128)S(1)}, u32[]{:S(2)}, u32[]{:S(2)}) collective-permute-start(f32[1,64,4096]{2,1,0:T(8,128)S(1)} %bitcast.158), channel_id=1, source_target_pairs={{0,124},{4,0},{8,4},{12,8},{16,12},{20,16},{24,20},{28,24},{32,28}... | collective-permute-start | bytes 3145736 | tf_op jit(solution)/shard_map/ppermute | solution.py:20
  77.8 1.0 copy-start.3
  78.8 28.1 %collective-permute-start.5 = (f32[1,64,4096]{2,1,0:T(8,128)S(1)}, f32[1,64,4096]{2,1,0:T(8,128)}, u32[]{:S(2)}, u32[]{:S(2)}) collective-permute-start(f32[1,64,4096]{2,1,0:T(8,128)S(1)} %collective-permute-done.4), channel_id=1, source_target_pairs={{0,124},{4,0},{8,4},{12,8},{16,12},{20,16},{24,20},{28,24},{32,28}... | collective-permute-start | bytes 3145736 | tf_op jit(solution)/shard_map/ppermute | solution.py:20
  106.9 111.3 %collective-permute-start.6 = (f32[1,64,4096]{2,1,0:T(8,128)}, f32[1,64,4096]{2,1,0:T(8,128)}, u32[]{:S(2)}, u32[]{:S(2)}) collective-permute-start(f32[1,64,4096]{2,1,0:T(8,128)} %collective-permute-done.5), channel_id=1, source_target_pairs={{0,124},{4,0},{8,4},{12,8},{16,12},{20,16},{24,20},{28,24},{32,28}... | collective-permute-start | bytes 3145736 | tf_op jit(solution)/shard_map/ppermute | solution.py:20
  115.9 2.3 copy-start.4
  118.4 1.0 copy-start.5
  168.2 191.9 %collective-permute-start.7 = (f32[1,64,4096]{2,0,1:T(1,128)}, f32[1,64,4096]{2,0,1:T(1,128)}, u32[]{:S(2)}, u32[]{:S(2)}) collective-permute-start(f32[1,64,4096]{2,0,1:T(1,128)} %copy.9), channel_id=1, source_target_pairs={{0,4},{4,8},{8,12},{12,16},{16,20},{20,24},{24,28},{28,32},{32,36}... | collective-permute-start | bytes 3145736 | tf_op jit(solution)/shard_map/ppermute | solution.py:20
  218.2 142.0 %collective-permute-start.8 = (f32[1,64,4096]{2,0,1:T(1,128)}, f32[1,64,4096]{2,0,1:T(1,128)}, u32[]{:S(2)}, u32[]{:S(2)}) collective-permute-start(f32[1,64,4096]{2,0,1:T(1,128)} %copy.11), channel_id=1, source_target_pairs={{0,8},{4,12},{8,16},{12,20},{16,24},{20,28},{24,32},{28,36},{32,40... | collective-permute-start | bytes 3145736 | tf_op jit(solution)/shard_map/ppermute | solution.py:20
  268.1 92.0 %collective-permute-start.9 = (f32[1,64,4096]{2,0,1:T(1,128)}, f32[1,64,4096]{2,0,1:T(1,128)}, u32[]{:S(2)}, u32[]{:S(2)}) collective-permute-start(f32[1,64,4096]{2,0,1:T(1,128)} %copy.12), channel_id=1, source_target_pairs={{0,12},{4,16},{8,20},{12,24},{16,28},{20,32},{24,36},{28,40},{32,4... | collective-permute-start | bytes 3145736 | tf_op jit(solution)/shard_map/ppermute | solution.py:20
  354.3 2.2 copy-start.2
  366.7 18.0 %all-to-all-start.2 = ((f32[1,1,64,4096]{3,1,0,2:T(1,128)}), f32[1,1,64,4096]{3,1,0,2:T(1,128)S(1)}, u32[]{:S(2)}, u32[]{:S(2)}) async-start(f32[1,1,64,4096]{3,1,0,2:T(1,128)} %add_bitcast_fusion), calls=%async_computation.2 | async-start | bytes 2097152 | tf_op jit(solution)/shard_map/all_to_all | solution.py:142
  384.7 19.9 %all-to-all-start.1 = ((f32[1,1,64,4096]{3,1,0,2:T(1,128)}), f32[1,1,64,4096]{3,1,0,2:T(1,128)S(1)}, u32[]{:S(2)}, u32[]{:S(2)}) async-start(f32[1,1,64,4096]{3,1,0,2:T(1,128)} %add_bitcast_fusion.1), calls=%async_computation.1 | async-start | bytes 2097152 | tf_op jit(solution)/shard_map/all_to_all | solution.py:141
  388.2 18.1 %collective-permute-start.13 = (f32[1,16,4096]{2,0,1:T(1,128)S(1)}, f32[1,16,4096]{2,0,1:T(1,128)S(1)}, u32[]{:S(2)}, u32[]{:S(2)}) collective-permute-start(f32[1,16,4096]{2,0,1:T(1,128)S(1)} %slice_bitcast_fusion), channel_id=1, source_target_pairs={{0,52},{4,56},{8,60},{12,64},{16,68},{20,72},{24,76},{28,80},{32,8... | collective-permute-start | bytes 786440 | tf_op jit(solution)/shard_map/ppermute | solution.py:20
  400.1 15.4 %collective-permute-start.12 = (f32[1,16,4096]{2,0,1:T(1,128)}, f32[1,16,4096]{2,0,1:T(1,128)S(1)}, u32[]{:S(2)}, u32[]{:S(2)}) collective-permute-start(f32[1,16,4096]{2,0,1:T(1,128)} %get-tuple-element.342), channel_id=1, source_target_pairs={{0,36},{4,40},{8,44},{12,48},{16,52},{20,56},{24,60},{28,64},{32,6... | collective-permute-start | bytes 786440 | tf_op jit(solution)/shard_map/ppermute | solution.py:20
  400.1 30.8 %collective-permute-start.11 = (f32[1,16,4096]{2,0,1:T(1,128)}, f32[1,16,4096]{2,0,1:T(1,128)S(1)}, u32[]{:S(2)}, u32[]{:S(2)}) collective-permute-start(f32[1,16,4096]{2,0,1:T(1,128)} %get-tuple-element.341), channel_id=1, source_target_pairs={{0,20},{4,24},{8,28},{12,32},{16,36},{20,40},{24,44},{28,48},{32,5... | collective-permute-start | bytes 786440 | tf_op jit(solution)/shard_map/ppermute | solution.py:20
  403.9 31.6 %collective-permute-start.10 = (f32[1,16,4096]{2,0,1:T(1,128)S(1)}, f32[1,16,4096]{2,0,1:T(1,128)}, u32[]{:S(2)}, u32[]{:S(2)}) collective-permute-start(f32[1,16,4096]{2,0,1:T(1,128)S(1)} %slice_bitcast_fusion.3), channel_id=1, source_target_pairs={{0,4},{4,8},{8,12},{12,16},{16,20},{20,24},{24,28},{28,32},{32,36}... | collective-permute-start | bytes 786440 | tf_op jit(solution)/shard_map/ppermute | solution.py:20
where the time goes:
time: 444 us; the launch traced here: 438 us
  matrix products  144 us (32%)
  waiting for transfers between devices  96.9 us (22%)
  local copies, waits for them, and re-layouts  78.5 us (18%)
  starting transfers between devices  56.6 us (13%)
  other arithmetic  38.5 us (9%)
  blocking collectives  18 us (4%)
    dot_general x30, matrix products, convolve(): jnp.einsum('ka,qabc->qbck', cas_matrix, cube_view, precision=HIGHEST_PREC...  144 us
    ppermute x14, waiting for transfers between devices, shifted(): lax.ppermute(shard, axis, [(i, (i + by) % length) for i in range(length)])  89.2 us
    ppermute x14, starting transfers between devices, shifted(): lax.ppermute(shard, axis, [(i, (i + by) % length) for i in range(length)])  49.6 us
    dot_general x5, local copies, waits for them, and re-layouts, convolve(): jnp.einsum('ka,qabc->qbck', cas_matrix, cube_view, precision=HIGHEST_PREC...  19.7 us
    cond x8, local copies, waits for them, and re-layouts, visit_terms(): return lax.cond(has_work, full_work, no_work, 0)  19.2 us
    all_to_all x1, blocking collectives, body(): lax.all_to_all(pieces, 'pair', split_axis=0, concat_axis=2, tiled=True)[0]  18 us
    another operation x5, local copies, waits for them, and re-layouts  16 us
    mul x5, local copies, waits for them, and re-layouts, row_step(): own_weight * potential * partner_block  13.8 us
  transfers between devices with their start and end apart: 16, of which 10 were waited for; matrix products, arithmetic and copies ran while one was open for 57% of the time, Pallas kernels for 0%

commit v1 on v0

v1 whole, which is shorter than its diff:
```python
import functools
import math

import jax
import jax.numpy as jnp
import ml_dtypes
import numpy as np
from jax import lax
from jax.experimental import pallas as pl
from jax.experimental.pallas import tpu as pltpu
from jax.sharding import PartitionSpec as P

NX = NY = NZ = 64
NYZ = NY * NZ
CELL_LENGTH = 46.92
SCREEN_OMEGA = 0.11
BF16 = jnp.bfloat16
F32 = jnp.float32
MESH = pl.DeviceIdType.MESH

ELEMENTS = [[((0, 1, 0), (0, 1, 0), None), ((0, 0, 1), (0, 0, 1), None), ((1, 3, 0), (1, 3, 0), None), ((2, 0, 1), (2, 0, 1), None), ((3, 0, 0), (3, 0, 0), None)], [((1, 0, 0), (1, 0, 0), None), ((3, 0, 0), (3, 2, 0), 0), ((1, 0, 1), (1, 0, 1), None), ((0, 2, 0), (0, 2, 0), None), ((0, 0, 1), (0, 0, 1), None)]]
EARLY = [4, 4]
EARLY_BACK = [[1, 3], [1, 2]]
LATE_BACK = [[0, 2, 4], [0, 3, 4]]
PAIRS = [[[[(3, 4, 3, 4, None, 0), (2, 3, 2, 3, None, 0)], [(0, 3, 0, 3, None, 0), (3, 5, 3, 5, None, 0)]], [[(2, 1, 2, 1, None, 0), (4, 1, 4, 1, None, 0)], [(0, 1, 0, 1, None, 0), (5, 1, 5, 1, None, 0)]]], [[[(1, 2, 1, 2, 0, 0), (3, 2, 3, 2, 0, 0)], [(0, 1, 0, 1, None, 0), (4, 1, 4, 1, None, 0)]], [[(0, 3, 0, 3, None, 0), (4, 3, 4, 3, None, 0)], [(4, 0, 4, 5, 1, 0), (0, 5, 0, 5, None, 1)]]]]
K = max(len(ELEMENTS[0]), len(ELEMENTS[1]))
JC = 8
YC = 2 * JC


def cas_matrix():
    counter = np.arange(64)
    angles = 2.0 * math.pi * (np.outer(counter, counter) % 64) / 64
    return np.cos(angles) + np.sin(angles)


def split_constant(matrix):
    high = matrix.astype(ml_dtypes.bfloat16)
    low = (matrix - high.astype(np.float64)).astype(ml_dtypes.bfloat16)
    return high, low


def lane_matrix():
    high, low = split_constant(np.kron(np.eye(2), cas_matrix()))
    row = np.concatenate([high, low], axis=1)
    return np.concatenate([row, row], axis=0)


def sublane_matrix():
    high, low = split_constant(cas_matrix())
    return np.concatenate([np.concatenate([high, high], 1), np.concatenate([low, low], 1)], 0)


def screened_table():
    counter = np.arange(64)
    wave = np.minimum(counter, 64 - counter) * (2.0 * math.pi / CELL_LENGTH)
    square = wave[:, None, None] ** 2 + wave[None, :, None] ** 2 + wave[None, None, :] ** 2
    guarded = np.where(square > 0.0, square, 1.0)
    screened = 4.0 * math.pi / guarded * -np.expm1(-guarded / (4.0 * SCREEN_OMEGA**2))
    table = np.where(square > 0.0, screened, 0.0) * (-1.0 / (NX * NY * NZ))
    return np.concatenate([table, table], axis=2).astype(np.float32)


def dot(a, b):
    return jnp.dot(a, b, preferred_element_type=F32)


def halves(v):
    high = v.astype(BF16)
    low = (v - high.astype(F32)).astype(BF16)
    return high, low


def along_lanes(v, weights):
    out = dot(jnp.concatenate(halves(v), axis=1), weights)
    return out[:, :128] + out[:, 128:]


def along_rows(v, weights):
    out = dot(weights, jnp.concatenate(halves(v), axis=0))
    return out[:64] + out[64:]


def rows_to_lanes(v, count):
    return jnp.concatenate([v[64 * i : 64 * i + 64] for i in range(count)], axis=1)


def lanes_to_rows(v, count):
    return jnp.concatenate([v[:, 128 * i : 128 * i + 128] for i in range(count)], axis=0)


class Place:
    def __init__(self):
        band = lax.axis_index("band")
        pair = lax.axis_index("pair")
        self.z, self.y, self.h = band // 8, (band // 2) % 4, band % 2
        self.l, self.c = pair // 2, pair % 2
        self.band = band

    def shifted(self, u, sign):
        z = (self.z + 4 + sign * u[0]) % 4
        y = (self.y + 4 + sign * u[1]) % 4
        h = (self.h + u[2]) % 2
        return z, y, h

    def band_at(self, u, sign):
        z, y, h = self.shifted(u, sign)
        return (z * 4 + y) * 2 + h

    def phase_at(self, phase, u, sign):
        z, y, _ = self.shifted(u, sign)
        return (z // 2) if phase == 0 else (y // 2)


def variants(element):
    first, second, phase = element
    if phase is None:
        return [(first, None, 0)]
    return [(first, phase, 0), (second, phase, 1)]


def hosts(place):
    found = []
    for host_l in (0, 1):
        for e, element in enumerate(ELEMENTS[host_l]):
            for v, (u, phase, value) in enumerate(variants(element)):
                here = host_l if u[2] == 0 else 1 - host_l
                condition = place.l == here
                if phase is not None:
                    condition = condition & (place.phase_at(phase, u, -1) == value)
                found.append((host_l, e, u, condition))
    return found


def wants(place):
    found = []
    for host_l in (0, 1):
        for e, element in enumerate(ELEMENTS[host_l]):
            for v, (u, phase, value) in enumerate(variants(element)):
                condition = place.l == host_l
                if phase is not None:
                    condition = condition & (place.phase_at(phase, (0, 0, 0), 1) == value)
                there = host_l if u[2] == 0 else 1 - host_l
                found.append((host_l, e, u, there, condition))
    return found


def kernel(orb_ref, keep_ref, wz_ref, wr_ref, table_hbm, out_ref,
           slots, acc, xbuf, rbuf, fbuf, spect, table,
           local_sem, d_send, d_recv, f_send, f_recv, x_send, x_recv, r_send, r_recv, s_sem):
    at = Place()
    l, c = at.l, at.c
    sibling = (at.band, 2 * l + 1 - c)
    twin = (at.band, 2 * (1 - l) + c)

    def pick(values):
        out = 0
        for (pl_, pc_), value in values.items():
            if value != 0:
                out = out + value * ((l == pl_) & (c == pc_)).astype(jnp.int32)
        return out

    own_copy = pltpu.make_async_copy(orb_ref, slots.at[0], local_sem.at[0])
    own_copy.start()
    table_copy = pltpu.make_async_copy(table_hbm, table, local_sem.at[1])
    table_copy.start()

    barrier = pltpu.get_barrier_semaphore()
    peers = 2
    pl.semaphore_signal(barrier, inc=1, device_id=sibling, device_id_type=MESH)
    pl.semaphore_signal(barrier, inc=1, device_id=twin, device_id_type=MESH)
    host_list, want_list = hosts(at), wants(at)
    for host_l, e, u, condition in host_list:
        peers = peers + condition.astype(jnp.int32)
        device = (at.band_at(u, -1), 2 * host_l + c)

        @pl.when(condition)
        def _():
            pl.semaphore_signal(barrier, inc=1, device_id=device, device_id_type=MESH)

    for host_l, e, u, there, condition in want_list:
        peers = peers + condition.astype(jnp.int32)
        device = (at.band_at(u, 1), 2 * there + c)

        @pl.when(condition)
        def _():
            pl.semaphore_signal(barrier, inc=1, device_id=device, device_id_type=MESH)

    for e in range(1, K + 1):
        acc[e] = jnp.zeros(acc.shape[1:], F32)
    own_copy.wait()
    pl.semaphore_wait(barrier, peers)

    my_rows = pl.ds(pl.multiple_of(32 * c, 32), 32)

    def orbital_out(host_l, e, u):
        return pltpu.make_async_remote_copy(
            src_ref=slots.at[0, my_rows], dst_ref=slots.at[e + 1, my_rows],
            send_sem=d_send.at[host_l * K + e], recv_sem=d_recv.at[e],
            device_id=(at.band_at(u, -1), 2 * host_l + c), device_id_type=MESH)

    for host_l, e, u, condition in sorted(host_list, key=lambda t: t[1]):

        @pl.when(condition)
        def _():
            orbital_out(host_l, e, u).start()

    def forward(e):
        return pltpu.make_async_remote_copy(
            src_ref=slots.at[e + 1, my_rows], dst_ref=slots.at[e + 1, my_rows],
            send_sem=f_send.at[e], recv_sem=f_recv.at[e], device_id=sibling, device_id_type=MESH)

    def for_elements(first, body):
        for host_l in (0, 1):
            chosen = [e for e in range(len(ELEMENTS[host_l])) if (e < EARLY[host_l]) == first]

            @pl.when(l == host_l)
            def _():
                for e in chosen:
                    body(e)

    def pass_on(e):
        orbital_out(0, e, (0, 0, 0)).wait_recv()
        forward(e).start()

    def pass_done(e):
        forward(e).wait()

    low_lanes = lax.broadcasted_iota(jnp.int32, (64, 128), 1) < 64

    def lanes_of(i):
        return pl.ds(pl.multiple_of(i * (128 * JC), 128 * JC), 128 * JC)

    def transform(pairs, update, between):
        wz, wr = wz_ref[...], wr_ref[...]
        (p0, q0), (p1, q1) = pairs

        def first(i, carry):
            lanes = lanes_of(i)
            d0 = slots[p0, :, lanes] * slots[q0, :, lanes]
            d1 = slots[p1, :, lanes] * slots[q1, :, lanes]
            tiles = []
            for j in range(JC):
                t0, t1 = d0[:, 128 * j : 128 * j + 128], d1[:, 128 * j : 128 * j + 128]
                tiles.append(jnp.where(low_lanes, t0, pltpu.roll(t1, 64, 1)))
                tiles.append(jnp.where(low_lanes, pltpu.roll(t0, 64, 1), t1))
            v = along_lanes(jnp.concatenate(tiles, axis=0), wz)
            v = along_rows(rows_to_lanes(v, YC), wr)
            spect[pl.ds(pl.multiple_of(i * (64 * YC), 64 * YC), 64 * YC), :] = lanes_to_rows(v, YC)
            return carry

        def second(i, carry):
            rows = [pl.ds(i * YC + k, 64, stride=64) for k in range(YC)]
            v = along_rows(jnp.concatenate([spect[r, :] for r in rows], axis=1), wr)
            scale = jnp.concatenate([table[i * YC + k] for k in range(YC)], axis=1)
            v = along_rows(v * scale, wr)
            for k in range(YC):
                spect[rows[k], :] = v[:, 128 * k : 128 * k + 128]
            return carry

        def third(i, carry):
            v = spect[pl.ds(pl.multiple_of(i * (64 * YC), 64 * YC), 64 * YC), :]
            v = along_rows(rows_to_lanes(v, YC), wr)
            v = along_lanes(lanes_to_rows(v, YC), wz)
            v0, v1 = [], []
            for j in range(JC):
                even, odd = v[128 * j : 128 * j + 64], v[128 * j + 64 : 128 * j + 128]
                v0.append(jnp.where(low_lanes, even, pltpu.roll(odd, 64, 1)))
                v1.append(jnp.where(low_lanes, pltpu.roll(even, 64, 1), odd))
            update(lanes_of(i), jnp.concatenate(v0, axis=1), jnp.concatenate(v1, axis=1))
            return carry

        lax.fori_loop(0, 64 // YC, first, 0)
        lax.fori_loop(0, 64 // YC, second, 0)
        between()
        lax.fori_loop(0, 64 // YC, third, 0)

    def keep_at(i, j):
        return keep_ref[i, j].astype(F32)

    self_keep = keep_at(at.band, at.band)

    def self_update(lanes, v0, v1):
        orbital = slots[0, :, lanes]
        for s in range(4):
            rows = slice(16 * s, 16 * s + 16)
            mine = self_keep * (2 * l + c == s).astype(F32)
            acc[0, s % 2, s // 2, :, lanes] = (mine * v0[rows]) * orbital[rows]

    def pair_batch(b, between):
        pairs, scales = [], []
        for k in range(2):
            entries = {(pl_, pc_): PAIRS[pl_][pc_][b][k] for pl_ in (0, 1) for pc_ in (0, 1)}

            def value(field):
                return pick({key: field(entry) for key, entry in entries.items()})

            phase = (value(lambda t: int(t[4] == 0)) * (at.z // 2)
                     + value(lambda t: int(t[4] == 1)) * (at.y // 2))

            def both(field):
                v0 = value(lambda t: field(t, 0))
                return v0 + phase * (value(lambda t: field(t, 1)) - v0)

            p = both(lambda t, w: t[2 * w])
            q = both(lambda t, w: t[2 * w + 1])

            def band_of(which):
                def part(axis):
                    def get(host_l, t, w):
                        index = t[2 * w + which]
                        if index == 0:
                            return 0
                        element = ELEMENTS[host_l][index - 1]
                        return element[1 if (element[2] is not None and w == 1) else 0][axis]

                    def table_of(w):
                        return pick({key: get(key[0], entry, w) for key, entry in entries.items()})

                    v0 = table_of(0)
                    return v0 + phase * (table_of(1) - v0)

                z = (at.z + part(0)) % 4
                y = (at.y + part(1)) % 4
                h = (at.h + part(2)) % 2
                return (z * 4 + y) * 2 + h

            weight = keep_at(band_of(0), band_of(1))
            unused = value(lambda t: int(t[5])) * at.h
            pairs.append((p, q))
            scales.append(weight * (jnp.int32(1) - unused).astype(F32))

        def update(lanes, v0, v1):
            for (p, q), scale, v in zip(pairs, scales, (v0, v1)):
                scaled = scale * v
                to_p = scaled * slots[q, :, lanes]
                to_q = scaled * slots[p, :, lanes]
                for target, term in ((p, to_p), (q, to_q)):
                    for s in range(4):
                        acc[target, s % 2, s // 2, :, lanes] += term[16 * s : 16 * s + 16]

        transform(pairs, update, between)

    def exchange(e):
        return pltpu.make_async_remote_copy(
            src_ref=acc.at[e, 1 - c], dst_ref=xbuf.at[e],
            send_sem=x_send.at[e], recv_sem=x_recv.at[e], device_id=sibling, device_id_type=MESH)

    def send_back(host_l, e, u, there):
        return pltpu.make_async_remote_copy(
            src_ref=acc.at[e + 1, c], dst_ref=rbuf.at[host_l * K + e],
            send_sem=r_send.at[e], recv_sem=r_recv.at[host_l * K + e],
            device_id=(at.band_at(u, 1), 2 * there + c), device_id_type=MESH)

    def return_all(chosen):
        for host_l in (0, 1):
            mine = chosen[host_l]

            @pl.when(l == host_l)
            def _():
                for e in mine:
                    exchange(e + 1).start()

        for host_l in (0, 1):
            mine = chosen[host_l]

            @pl.when(l == host_l)
            def _():
                for e in mine:
                    exchange(e + 1).wait_recv()
                    acc[e + 1, c] += xbuf[e + 1]
                    for w_l, w_e, u, there, condition in want_list:
                        if (w_l, w_e) == (host_l, e):

                            @pl.when(condition)
                            def _():
                                send_back(w_l, w_e, u, there).start()

    table_copy.wait()
    for_elements(True, pass_on)
    transform([(0, 0), (0, 0)], self_update, lambda: None)
    for_elements(True, pass_done)
    pair_batch(0, lambda: for_elements(False, pass_on))
    for_elements(False, pass_done)
    return_all(EARLY_BACK)
    pair_batch(1, lambda: None)
    exchange(0).start()
    return_all(LATE_BACK)
    exchange(0).wait_recv()
    acc[0, c] += xbuf[0]

    for host_l, e, u, condition in host_list:

        @pl.when(condition)
        def _():
            send_back(host_l, e, u, 0).wait_recv()
            acc[0, c] += rbuf[host_l * K + e]

    swap = pltpu.make_async_remote_copy(
        src_ref=acc.at[0, c, 1 - l], dst_ref=fbuf, send_sem=s_sem.at[0], recv_sem=s_sem.at[1],
        device_id=twin, device_id_type=MESH)
    swap.start()
    swap.wait()
    out_ref[...] = acc[0, c, l] + fbuf[...]

    exchange(0).wait_send()
    for host_l, e, u, condition in host_list:

        @pl.when(condition)
        def _():
            orbital_out(host_l, e, u).wait_send()

    for host_l, e, u, there, condition in want_list:

        @pl.when(condition)
        def _():
            exchange(e + 1).wait_send()
            send_back(host_l, e, u, there).wait_send()


def body(orbitals, pair_keep, wz, wr, table):
    dma = pltpu.SemaphoreType.DMA
    out = pl.pallas_call(
        kernel,
        name="exchange",
        out_shape=jax.ShapeDtypeStruct((16, NYZ), F32),
        in_specs=[
            pl.BlockSpec(memory_space=pl.ANY),
            pl.BlockSpec(memory_space=pltpu.SMEM),
            pl.BlockSpec(memory_space=pltpu.VMEM),
            pl.BlockSpec(memory_space=pltpu.VMEM),
            pl.BlockSpec(memory_space=pl.ANY),
        ],
        out_specs=pl.BlockSpec(memory_space=pltpu.VMEM),
        scratch_shapes=[
            pltpu.VMEM((K + 1, NX, NYZ), F32),
            pltpu.VMEM((K + 1, 2, 2, 16, NYZ), F32),
            pltpu.VMEM((K + 1, 2, 16, NYZ), F32),
            pltpu.VMEM((2 * K, 2, 16, NYZ), F32),
            pltpu.VMEM((16, NYZ), F32),
            pltpu.VMEM((64 * 64, 128), F32),
            pltpu.VMEM((64, 64, 128), F32),
            dma((2,)),
            dma((2 * K,)), dma((K,)),
            dma((K,)), dma((K,)),
            dma((K + 1,)), dma((K + 1,)),
            dma((K,)), dma((2 * K,)),
            dma((2,)),
        ],
        compiler_params=pltpu.CompilerParams(
            collective_id=0, has_side_effects=True, vmem_limit_bytes=56 << 20),
    )(orbitals.reshape(NX, NYZ), pair_keep, wz, wr, table)
    return out.reshape(1, 16, NYZ)


def solution(mesh):
    constants = (lane_matrix(), sublane_matrix(), screened_table())

    def call(orbitals, pair_keep):
        return body(orbitals, pair_keep, *[jnp.asarray(x) for x in constants])

    return jax.shard_map(
        call,
        mesh=mesh,
        in_specs=(P("band", None, None), P()),
        out_specs=P("band", "pair", None),
        check_vma=False,
    )
```

time: 444 us -> 96.8 us (0.22)
  the two profiles are of different devices: /device:TPU:32 before, /device:TPU:0 now
where the time goes in v1:
time: 96.8 us; the launch traced here: 95.5 us
  Pallas kernels  93.8 us (97%)
  local copies, waits for them, and re-layouts  1.67 us (2%)
    pallas_call x1, Pallas kernels, body(): pl.pallas_call(kernel, name='exchange', out_shape=jax.ShapeDtypeStruct((1...  93.8 us

profile of v1, /device:TPU:0, one launch (start us, length us, event | category | flops | bytes accessed | tf_op | source)
XLA Modules:
  0.0 95.5 jit_solution(7064597070100313666)
XLA Ops:
  0.0 93.8 %exchange.1 = f32[16,4096]{1,0:T(8,128)} custom-call(f32[64,4096]{1,0:T(8,128)} %bitcast.2, s32[32,32]{1,0:T(8,128)} %keep_ref.1, bf16[256,256]{1,0:T(8,128)(2,1)} %constant.6.clone.wz_ref, bf16[128,128]{1,0:T(8,128)(2,1)} %constant.7.clone.wr_ref, f32[64,64,128]{2,1,0:T(8,128)} %constant.8.clone.table_hbm), custom_call_target="tpu_custom_call" | custom-call | tf_op jit(solution)/shard_map/exchange/pallas_call | solution.py:423
  93.8 1.7 %copy.7 = f32[1,16,4096]{2,1,0:T(8,128)} copy(f32[1,16,4096]{2,1,0:T(8,128)} %bitcast.3) | data formatting | bytes 524288

commit v2 on v1

v2 whole, which is shorter than its diff:
```python
import functools
import math

import jax
import jax.numpy as jnp
import ml_dtypes
import numpy as np
from jax import lax
from jax.experimental import pallas as pl
from jax.experimental.pallas import tpu as pltpu
from jax.sharding import PartitionSpec as P

NX = NY = NZ = 64
NYZ = NY * NZ
CELL_LENGTH = 46.92
SCREEN_OMEGA = 0.11
BF16 = jnp.bfloat16
F32 = jnp.float32
MESH = pl.DeviceIdType.MESH

ELEMENTS = [[((0, 3, 0), (0, 3, 0), 0, None), ((1, 0, 1), (1, 0, 1), 0, None), ((3, 1, 0), (3, 1, 0), 0, None), ((0, 0, 1), (0, 0, 1), 0, None), ((1, 0, 0), (1, 0, 0), 0, None)], [((0, 2, 0), (0, 2, 0), 0, None), ((2, 0, 0), (2, 0, 1), 1, None), ((1, 0, 1), (1, 0, 1), 0, ((0, 0, 0), 0, 2)), ((3, 0, 0), (3, 0, 0), 0, None), ((0, 0, 1), (0, 0, 1), 0, None)]]
EARLY_NEAR = [[0, 1, 2], [0, 1]]
EARLY_FAR = [[], [2]]
LATE_NEAR = [[3, 4], [3, 4]]
LATE_FAR = [[], []]
BACK_EARLY = [[], [1, 2]]
BACK_EARLY_JOIN = [[1], []]
BACK_LATE = [[0, 2, 3, 4], [0, 3, 4]]
BACK_LATE_JOIN = [[], []]
PAIRS = [[[[(1, 0, 1, 0, 0, 0), (2, 3, 2, 3, 0, 0)], [(1, 4, 1, 4, 0, 0), (3, 4, 3, 4, 0, 0)]], [[(1, 2, 1, 2, 0, 0), (3, 0, 3, 0, 0, 0)], [(1, 5, 1, 5, 0, 0), (5, 3, 5, 3, 0, 0)]]], [[[(0, 2, 0, 2, 1, 0), (1, 2, 1, 2, 1, 0)], [(4, 0, 4, 0, 0, 0), (4, 5, 4, 5, 0, 0)]], [[(1, 3, 1, 3, 0, 0), (1, 0, 1, 0, 0, 2)], [(4, 1, 4, 1, 0, 0), (5, 1, 5, 0, 5, 0)]]]]
K = max(len(ELEMENTS[0]), len(ELEMENTS[1]))
JC = 8
YC = 2 * JC
CHUNK = 128 * JC


def cas_matrix():
    counter = np.arange(64)
    angles = 2.0 * math.pi * (np.outer(counter, counter) % 64) / 64
    return np.cos(angles) + np.sin(angles)


def split_constant(matrix):
    high = matrix.astype(ml_dtypes.bfloat16)
    low = (matrix - high.astype(np.float64)).astype(ml_dtypes.bfloat16)
    return high, low


def lane_matrix():
    high, low = split_constant(np.kron(np.eye(2), cas_matrix()))
    row = np.concatenate([high, low], axis=1)
    return np.concatenate([row, row], axis=0)


def sublane_matrix():
    high, low = split_constant(cas_matrix())
    return np.concatenate([np.concatenate([high, high], 1), np.concatenate([low, low], 1)], 0)


def screened_table():
    counter = np.arange(64)
    wave = np.minimum(counter, 64 - counter) * (2.0 * math.pi / CELL_LENGTH)
    square = wave[:, None, None] ** 2 + wave[None, :, None] ** 2 + wave[None, None, :] ** 2
    guarded = np.where(square > 0.0, square, 1.0)
    screened = 4.0 * math.pi / guarded * -np.expm1(-guarded / (4.0 * SCREEN_OMEGA**2))
    table = np.where(square > 0.0, screened, 0.0) * (-1.0 / (NX * NY * NZ))
    return np.concatenate([table, table], axis=2).astype(np.float32)


def dot(a, b):
    return jnp.dot(a, b, preferred_element_type=F32)


def halves(v):
    high = v.astype(BF16)
    low = (v - high.astype(F32)).astype(BF16)
    return high, low


def along_lanes(v, weights):
    out = dot(jnp.concatenate(halves(v), axis=1), weights)
    return out[:, :128] + out[:, 128:]


def along_rows(v, weights):
    out = dot(weights, jnp.concatenate(halves(v), axis=0))
    return out[:64] + out[64:]


def rows_to_lanes(v, count):
    return jnp.concatenate([v[64 * i : 64 * i + 64] for i in range(count)], axis=1)


def lanes_to_rows(v, count):
    return jnp.concatenate([v[:, 128 * i : 128 * i + 128] for i in range(count)], axis=0)


class Place:
    def __init__(self):
        band = lax.axis_index("band")
        pair = lax.axis_index("pair")
        self.z, self.y, self.h = band // 8, (band // 2) % 4, band % 2
        self.l, self.c = pair // 2, pair % 2
        self.band = band

    def shifted(self, u, sign):
        z = (self.z + 4 + sign * u[0]) % 4
        y = (self.y + 4 + sign * u[1]) % 4
        h = (self.h + u[2]) % 2
        return z, y, h

    def band_at(self, u, sign):
        z, y, h = self.shifted(u, sign)
        return (z * 4 + y) * 2 + h

    def phase_at(self, mask, u, sign):
        z, y, h = self.shifted(u, sign)
        bits = (z // 2, y // 2, h)
        return sum(bit for k, bit in enumerate(bits) if mask >> k & 1) % 2


class Transfer:
    def __init__(self, place, l, e, step, from_l, slot, mask=0, value=0):
        self.l, self.e, self.step, self.from_l, self.slot = l, e, step, from_l, slot
        self.here, self.mine = place.l == from_l, place.l == l
        if mask:
            self.here = self.here & (place.phase_at(mask, step, -1) == value)
            self.mine = self.mine & (place.phase_at(mask, (0, 0, 0), 1) == value)


def transfers(place):
    found = []
    for l in (0, 1):
        for e, (first, second, mask, relay) in enumerate(ELEMENTS[l]):
            if relay is not None:
                found.append(Transfer(place, l, e, *relay))
                continue
            for value, u in enumerate((first, second) if mask else (first,)):
                from_l = l if u[2] == 0 else 1 - l
                found.append(Transfer(place, l, e, u, from_l, 0, mask, value))
    return found


def kernel(orb_ref, keep_ref, wz_ref, wr_ref, table_hbm, out_ref,
           slots, acc, xbuf, rbuf, fbuf, spect, table,
           local_sem, d_send, d_recv, f_send, f_recv, x_send, x_recv, r_send, r_recv, s_send, s_recv):
    at = Place()
    l, c = at.l, at.c
    sibling = (at.band, 2 * l + 1 - c)
    twin = (at.band, 2 * (1 - l) + c)

    def pick(values):
        out = 0
        for (pl_, pc_), value in values.items():
            if value != 0:
                out = out + value * ((l == pl_) & (c == pc_)).astype(jnp.int32)
        return out

    own_copy = pltpu.make_async_copy(orb_ref, slots.at[0], local_sem.at[0])
    own_copy.start()
    table_copy = pltpu.make_async_copy(table_hbm, table, local_sem.at[1])
    table_copy.start()

    barrier = pltpu.get_barrier_semaphore()
    peers = 2
    pl.semaphore_signal(barrier, inc=1, device_id=sibling, device_id_type=MESH)
    pl.semaphore_signal(barrier, inc=1, device_id=twin, device_id_type=MESH)
    moves = transfers(at)

    def child(move):
        return (at.band_at(move.step, -1), 2 * move.l + c)

    def parent(move):
        return (at.band_at(move.step, 1), 2 * move.from_l + c)

    for move in moves:
        peers = peers + move.here.astype(jnp.int32) + move.mine.astype(jnp.int32)

        @pl.when(move.here)
        def _():
            pl.semaphore_signal(barrier, inc=1, device_id=child(move), device_id_type=MESH)

        @pl.when(move.mine)
        def _():
            pl.semaphore_signal(barrier, inc=1, device_id=parent(move), device_id_type=MESH)

    for e in range(1, K + 1):
        acc[e] = jnp.zeros(acc.shape[1:], F32)
    own_copy.wait()
    pl.semaphore_wait(barrier, peers)

    my_rows = pl.ds(pl.multiple_of(32 * c, 32), 32)

    def chunk(i):
        return pl.ds(pl.multiple_of(i * CHUNK, CHUNK), CHUNK)

    everything = pl.ds(0, NYZ)

    def orbital_out(move, lanes, i=0):
        return pltpu.make_async_remote_copy(
            src_ref=slots.at[move.slot, my_rows, lanes],
            dst_ref=slots.at[move.e + 1, my_rows, lanes],
            send_sem=d_send.at[move.l * K + move.e], recv_sem=d_recv.at[move.e * 4 + i],
            device_id=child(move), device_id_type=MESH)

    def is_early(move):
        return move.e in EARLY_NEAR[move.l] or move.e in EARLY_FAR[move.l]

    for early in (True, False):
        for i in range(4):
            for move in moves:
                if move.slot == 0 and is_early(move) == early:

                    @pl.when(move.here)
                    def _():
                        orbital_out(move, chunk(i), i).start()

    def forward(e, lanes, i=0):
        return pltpu.make_async_remote_copy(
            src_ref=slots.at[e + 1, my_rows, lanes], dst_ref=slots.at[e + 1, my_rows, lanes],
            send_sem=f_send.at[e], recv_sem=f_recv.at[e * 4 + i],
            device_id=sibling, device_id_type=MESH)

    def for_chip(chosen, body):
        for chip in (0, 1):
            if chosen[chip]:

                @pl.when(l == chip)
                def _():
                    for e in chosen[chip]:
                        body(chip, e)

    def pass_on(chosen, i):
        def one(chip, e):
            arriving = [move for move in moves if (move.l, move.e) == (chip, e)][0]
            orbital_out(arriving, chunk(i), i).wait_recv()
            forward(e, chunk(i), i).start()
            for move in moves:
                if (move.from_l, move.slot) == (chip, e + 1):
                    orbital_out(move, chunk(i), i).start()

        for_chip(chosen, one)

    def passed_on(chosen, i):
        for_chip(chosen, lambda chip, e: forward(e, chunk(i), i).wait_recv())

    low_lanes = lax.broadcasted_iota(jnp.int32, (64, 128), 1) < 64

    def lanes_of(i):
        return chunk(i)

    def transform(pairs, update, before=None, middle=None, after=None):
        wz, wr = wz_ref[...], wr_ref[...]
        (p0, q0), (p1, q1) = pairs

        def first(i, carry):
            if before is not None:
                before(i)
            lanes = lanes_of(i)
            d0 = slots[p0, :, lanes] * slots[q0, :, lanes]
            d1 = slots[p1, :, lanes] * slots[q1, :, lanes]
            tiles = []
            for j in range(JC):
                t0, t1 = d0[:, 128 * j : 128 * j + 128], d1[:, 128 * j : 128 * j + 128]
                tiles.append(jnp.where(low_lanes, t0, pltpu.roll(t1, 64, 1)))
                tiles.append(jnp.where(low_lanes, pltpu.roll(t0, 64, 1), t1))
            v = along_lanes(jnp.concatenate(tiles, axis=0), wz)
            v = along_rows(rows_to_lanes(v, YC), wr)
            spect[pl.ds(pl.multiple_of(i * (64 * YC), 64 * YC), 64 * YC), :] = lanes_to_rows(v, YC)
            return carry

        def second(i, carry):
            if middle is not None:
                middle(i)
            rows = [pl.ds(i * YC + k, 64, stride=64) for k in range(YC)]
            v = along_rows(jnp.concatenate([spect[r, :] for r in rows], axis=1), wr)
            scale = jnp.concatenate([table[i * YC + k] for k in range(YC)], axis=1)
            v = along_rows(v * scale, wr)
            for k in range(YC):
                spect[rows[k], :] = v[:, 128 * k : 128 * k + 128]
            return carry

        def third(i, carry):
            v = spect[pl.ds(pl.multiple_of(i * (64 * YC), 64 * YC), 64 * YC), :]
            v = along_rows(rows_to_lanes(v, YC), wr)
            v = along_lanes(lanes_to_rows(v, YC), wz)
            v0, v1 = [], []
            for j in range(JC):
                even, odd = v[128 * j : 128 * j + 64], v[128 * j + 64 : 128 * j + 128]
                v0.append(jnp.where(low_lanes, even, pltpu.roll(odd, 64, 1)))
                v1.append(jnp.where(low_lanes, pltpu.roll(even, 64, 1), odd))
            update(lanes_of(i), jnp.concatenate(v0, axis=1), jnp.concatenate(v1, axis=1))
            if after is not None:
                after(i)
            return carry

        lax.fori_loop(0, 64 // YC, first, 0)
        lax.fori_loop(0, 64 // YC, second, 0)
        lax.fori_loop(0, 64 // YC, third, 0)

    def keep_at(i, j):
        return keep_ref[i, j].astype(F32)

    self_keep = keep_at(at.band, at.band)

    def self_update(lanes, v0, v1):
        orbital = slots[0, :, lanes]
        for s in range(4):
            rows = slice(16 * s, 16 * s + 16)
            mine = self_keep * (2 * l + c == s).astype(F32)
            acc[0, s % 2, s // 2, :, lanes] = (mine * v0[rows]) * orbital[rows]

    def pair_batch(b, before, middle, after):
        pairs, scales = [], []
        for k in range(2):
            entries = {(pl_, pc_): PAIRS[pl_][pc_][b][k] for pl_ in (0, 1) for pc_ in (0, 1)}

            def value(field):
                return pick({key: field(entry) for key, entry in entries.items()})

            bits = (at.z // 2, at.y // 2, at.h)
            phase = sum(value(lambda t: t[4] >> n & 1) * bits[n] for n in range(3)) % 2
            unused = sum(value(lambda t: t[5] >> n & 1) * bits[n] for n in range(3)) % 2

            def both(field):
                v0 = value(lambda t: field(t, 0))
                return v0 + phase * (value(lambda t: field(t, 1)) - v0)

            p = both(lambda t, w: t[2 * w])
            q = both(lambda t, w: t[2 * w + 1])

            def band_of(which):
                def part(axis):
                    def get(host_l, t, w):
                        index = t[2 * w + which]
                        if index == 0:
                            return 0
                        element = ELEMENTS[host_l][index - 1]
                        return element[1 if (element[2] and w == 1) else 0][axis]

                    def table_of(w):
                        return pick({key: get(key[0], entry, w) for key, entry in entries.items()})

                    v0 = table_of(0)
                    return v0 + phase * (table_of(1) - v0)

                z = (at.z + part(0)) % 4
                y = (at.y + part(1)) % 4
                h = (at.h + part(2)) % 2
                return (z * 4 + y) * 2 + h

            weight = keep_at(band_of(0), band_of(1))
            pairs.append((p, q))
            scales.append(weight * (jnp.int32(1) - unused).astype(F32))

        def update(lanes, v0, v1):
            for (p, q), scale, v in zip(pairs, scales, (v0, v1)):
                scaled = scale * v
                to_p = scaled * slots[q, :, lanes]
                to_q = scaled * slots[p, :, lanes]
                for target, term in ((p, to_p), (q, to_q)):
                    for s in range(4):
                        acc[target, s % 2, s // 2, :, lanes] += term[16 * s : 16 * s + 16]

        transform(pairs, update, before, middle, after)

    def exchange(e, lanes, i=0):
        return pltpu.make_async_remote_copy(
            src_ref=acc.at[e, 1 - c, :, :, lanes], dst_ref=xbuf.at[e, :, :, lanes],
            send_sem=x_send.at[e], recv_sem=x_recv.at[e * 4 + i],
            device_id=sibling, device_id_type=MESH)

    def send_back(move, lanes, i=0):
        return pltpu.make_async_remote_copy(
            src_ref=acc.at[move.e + 1, c, :, :, lanes],
            dst_ref=rbuf.at[move.l * K + move.e, :, :, lanes],
            send_sem=r_send.at[move.e], recv_sem=r_recv.at[(move.l * K + move.e) * 4 + i],
            device_id=parent(move), device_id_type=MESH)

    def swap(lanes, i=0):
        return pltpu.make_async_remote_copy(
            src_ref=acc.at[0, c, 1 - l, :, lanes], dst_ref=fbuf.at[:, lanes],
            send_sem=s_send.at[0], recv_sem=s_recv.at[i], device_id=twin, device_id_type=MESH)

    def start_return(chosen, i):
        for_chip(chosen, lambda chip, e: exchange(e + 1, chunk(i), i).start())

    def collect(move, e, lanes, i):
        send_back(move, lanes, i).wait_recv()
        acc[e, c, :, :, lanes] += rbuf[move.l * K + move.e, :, :, lanes]

    def finish_return(chosen, i):
        lanes = chunk(i)

        def one(chip, e):
            exchange(e + 1, lanes, i).wait_recv()
            acc[e + 1, c, :, :, lanes] += xbuf[e + 1, :, :, lanes]
            for move in moves:
                if (move.from_l, move.slot) == (chip, e + 1):
                    collect(move, e + 1, lanes, i)
            for move in moves:
                if (move.l, move.e) == (chip, e):

                    @pl.when(move.mine)
                    def _():
                        send_back(move, lanes, i).start()

        for_chip(chosen, one)

    def at_step(i, step, *actions):
        @pl.when(i == step)
        def _():
            for action, *arguments in actions:
                action(*arguments)

    def first_before(i):
        at_step(i, 1, (pass_on, EARLY_FAR, 1))
        at_step(i, 2, (pass_on, EARLY_NEAR, 3), (pass_on, EARLY_FAR, 2))
        at_step(i, 3, (pass_on, EARLY_FAR, 3))
        passed_on(EARLY_NEAR, i)
        passed_on(EARLY_FAR, i)

    def first_middle(i):
        at_step(i, 0, (pass_on, LATE_NEAR, 0))

    def first_after(i):
        start_return(BACK_EARLY, i)
        start_return(BACK_EARLY_JOIN, i)

        @pl.when(i > 0)
        def _():
            finish_return(BACK_EARLY, i - 1)
            pass_on(LATE_NEAR, i)

    def second_before(i):
        pass_on(LATE_FAR, i)
        passed_on(LATE_NEAR, i)
        passed_on(LATE_FAR, i)

    def second_after(i):
        start_return(BACK_LATE, i)
        start_return(BACK_LATE_JOIN, i)
        exchange(0, chunk(i), i).start()
        finish_return(BACK_EARLY_JOIN, i)

        @pl.when(i > 0)
        def _():
            finish_return(BACK_LATE, i - 1)

    table_copy.wait()
    transform([(0, 0), (0, 0)], self_update)
    pass_on(EARLY_NEAR, 0)
    pass_on(EARLY_NEAR, 1)
    pass_on(EARLY_FAR, 0)
    pass_on(EARLY_NEAR, 2)
    pair_batch(0, first_before, first_middle, first_after)
    finish_return(BACK_EARLY, 3)
    pair_batch(1, second_before, None, second_after)
    finish_return(BACK_LATE, 3)

    def gather(i, carry):
        lanes = chunk(i)
        finish_return(BACK_LATE_JOIN, i)
        exchange(0, lanes, i).wait_recv()
        acc[0, c, :, :, lanes] += xbuf[0, :, :, lanes]
        for move in moves:
            if move.slot == 0:

                @pl.when(move.here)
                def _():
                    collect(move, 0, lanes, i)

        swap(lanes, i).start()
        return carry

    def finish(i, carry):
        lanes = chunk(i)
        swap(lanes, i).wait_recv()
        out_ref[:, lanes] = acc[0, c, l, :, lanes] + fbuf[:, lanes]
        return carry

    lax.fori_loop(0, 4, gather, 0)
    lax.fori_loop(0, 4, finish, 0)

    swap(everything).wait_send()
    exchange(0, everything).wait_send()
    elements = [range(len(ELEMENTS[0])), range(len(ELEMENTS[1]))]
    for_chip(elements, lambda chip, e: forward(e, everything).wait_send())
    for_chip(elements, lambda chip, e: exchange(e + 1, everything).wait_send())
    for move in moves:

        @pl.when(move.here)
        def _():
            orbital_out(move, everything).wait_send()

        @pl.when(move.mine)
        def _():
            send_back(move, everything).wait_send()


def body(orbitals, pair_keep, wz, wr, table):
    dma = pltpu.SemaphoreType.DMA
    out = pl.pallas_call(
        kernel,
        name="exchange",
        out_shape=jax.ShapeDtypeStruct((16, NYZ), F32),
        in_specs=[
            pl.BlockSpec(memory_space=pl.ANY),
            pl.BlockSpec(memory_space=pltpu.SMEM),
            pl.BlockSpec(memory_space=pltpu.VMEM),
            pl.BlockSpec(memory_space=pltpu.VMEM),
            pl.BlockSpec(memory_space=pl.ANY),
        ],
        out_specs=pl.BlockSpec(memory_space=pltpu.VMEM),
        scratch_shapes=[
            pltpu.VMEM((K + 1, NX, NYZ), F32),
            pltpu.VMEM((K + 1, 2, 2, 16, NYZ), F32),
            pltpu.VMEM((K + 1, 2, 16, NYZ), F32),
            pltpu.VMEM((2 * K, 2, 16, NYZ), F32),
            pltpu.VMEM((16, NYZ), F32),
            pltpu.VMEM((64 * 64, 128), F32),
            pltpu.VMEM((64, 64, 128), F32),
            dma((2,)),
            dma((2 * K,)), dma((4 * K,)),
            dma((K,)), dma((4 * K,)),
            dma((K + 1,)), dma((4 * K + 4,)),
            dma((K,)), dma((8 * K,)),
            dma((1,)), dma((4,)),
        ],
        compiler_params=pltpu.CompilerParams(
            collective_id=0, has_side_effects=True, vmem_limit_bytes=56 << 20),
    )(orbitals.reshape(NX, NYZ), pair_keep, wz, wr, table)
    return out.reshape(1, 16, NYZ)


def solution(mesh):
    constants = (lane_matrix(), sublane_matrix(), screened_table())

    def call(orbitals, pair_keep):
        return body(orbitals, pair_keep, *[jnp.asarray(x) for x in constants])

    return jax.shard_map(
        call,
        mesh=mesh,
        in_specs=(P("band", None, None), P()),
        out_specs=P("band", "pair", None),
        check_vma=False,
    )
```

time: 96.8 us -> 71.7 us (0.74); the launches traced: 95.5 us -> 71.6 us
  Pallas kernels: 93.8 us -> 69.9 us
    pallas_call x1, Pallas kernels: 93.8 us -> 69.9 us  [body(): pl.pallas_call(kernel, name='exchange', out_shape=jax.ShapeDtypeStruct((1...]
where the time goes in v2:
time: 71.7 us; the launch traced here: 71.6 us
  Pallas kernels  69.9 us (97%)
  local copies, waits for them, and re-layouts  1.67 us (2%)
    pallas_call x1, Pallas kernels, body(): pl.pallas_call(kernel, name='exchange', out_shape=jax.ShapeDtypeStruct((1...  69.9 us
    unnamed x1, local copies, waits for them, and re-layouts  1.67 us

profile of v2, /device:TPU:0, one launch (start us, length us, event | category | flops | bytes accessed | tf_op | source)
XLA Modules:
  0.0 71.6 jit_solution(7538501876214799823)
XLA Ops:
  0.0 69.9 %exchange.1 = f32[16,4096]{1,0:T(8,128)} custom-call(f32[64,4096]{1,0:T(8,128)} %bitcast.2, s32[32,32]{1,0:T(8,128)} %keep_ref.1, bf16[256,256]{1,0:T(8,128)(2,1)} %constant.6.clone.wz_ref, bf16[128,128]{1,0:T(8,128)(2,1)} %constant.7.clone.wr_ref, f32[64,64,128]{2,1,0:T(8,128)} %constant.8.clone.table_hbm), custom_call_target="tpu_custom_call" | custom-call | tf_op jit(solution)/shard_map/exchange/pallas_call | solution.py:503
  69.9 1.7 %copy.7 = f32[1,16,4096]{2,1,0:T(8,128)} copy(f32[1,16,4096]{2,1,0:T(8,128)} %bitcast.3) | data formatting | bytes 524288

commit v3 on v2

--- a/solution.py
+++ b/solution.py
@@ -18,16 +18,16 @@
 F32 = jnp.float32
 MESH = pl.DeviceIdType.MESH
 
-ELEMENTS = [[((0, 3, 0), (0, 3, 0), 0, None), ((1, 0, 1), (1, 0, 1), 0, None), ((3, 1, 0), (3, 1, 0), 0, None), ((0, 0, 1), (0, 0, 1), 0, None), ((1, 0, 0), (1, 0, 0), 0, None)], [((0, 2, 0), (0, 2, 0), 0, None), ((2, 0, 0), (2, 0, 1), 1, None), ((1, 0, 1), (1, 0, 1), 0, ((0, 0, 0), 0, 2)), ((3, 0, 0), (3, 0, 0), 0, None), ((0, 0, 1), (0, 0, 1), 0, None)]]
-EARLY_NEAR = [[0, 1, 2], [0, 1]]
-EARLY_FAR = [[], [2]]
-LATE_NEAR = [[3, 4], [3, 4]]
+ELEMENTS = [[((0, 2, 0), (0, 2, 0), 0, None), ((2, 0, 1), (2, 0, 0), 1, None), ((3, 1, 0), (3, 1, 0), 0, ((0, 0, 0), 1, 3)), ((3, 0, 0), (3, 0, 0), 0, None), ((0, 0, 1), (0, 0, 1), 0, None)], [((0, 3, 0), (0, 3, 0), 0, None), ((1, 0, 1), (1, 0, 1), 0, None), ((3, 1, 0), (3, 1, 0), 0, None), ((0, 2, 0), (0, 2, 0), 0, ((0, 0, 0), 0, 1)), ((0, 0, 1), (0, 0, 1), 0, None), ((1, 0, 0), (1, 0, 0), 0, None)]]
+EARLY_NEAR = [[0, 1], [0, 1, 2]]
+EARLY_FAR = [[2], [3]]
+LATE_NEAR = [[3, 4], [4, 5]]
 LATE_FAR = [[], []]
-BACK_EARLY = [[], [1, 2]]
-BACK_EARLY_JOIN = [[1], []]
-BACK_LATE = [[0, 2, 3, 4], [0, 3, 4]]
+BACK_EARLY = [[1, 2], [1, 3]]
+BACK_EARLY_JOIN = [[], []]
+BACK_LATE = [[0, 3, 4], [0, 2, 4, 5]]
 BACK_LATE_JOIN = [[], []]
-PAIRS = [[[[(1, 0, 1, 0, 0, 0), (2, 3, 2, 3, 0, 0)], [(1, 4, 1, 4, 0, 0), (3, 4, 3, 4, 0, 0)]], [[(1, 2, 1, 2, 0, 0), (3, 0, 3, 0, 0, 0)], [(1, 5, 1, 5, 0, 0), (5, 3, 5, 3, 0, 0)]]], [[[(0, 2, 0, 2, 1, 0), (1, 2, 1, 2, 1, 0)], [(4, 0, 4, 0, 0, 0), (4, 5, 4, 5, 0, 0)]], [[(1, 3, 1, 3, 0, 0), (1, 0, 1, 0, 0, 2)], [(4, 1, 4, 1, 0, 0), (5, 1, 5, 0, 5, 0)]]]]
+PAIRS = [[[[(3, 1, 3, 1, 0, 0), (1, 2, 1, 2, 1, 0)], [(4, 5, 4, 5, 0, 0), (1, 0, 1, 5, 3, 0)]], [[(3, 0, 3, 0, 0, 0), (0, 2, 0, 2, 1, 0)], [(4, 1, 4, 1, 0, 0), (5, 0, 5, 0, 0, 4)]]], [[[(1, 2, 1, 2, 0, 0), (2, 3, 2, 3, 0, 0)], [(1, 5, 1, 5, 0, 0), (0, 6, 0, 6, 0, 0)]], [[(1, 0, 1, 0, 0, 0), (4, 2, 4, 2, 0, 0)], [(3, 5, 3, 5, 0, 0), (6, 3, 6, 3, 0, 0)]]]]
 K = max(len(ELEMENTS[0]), len(ELEMENTS[1]))
 JC = 8
 YC = 2 * JC
@@ -184,8 +184,6 @@
         def _():
             pl.semaphore_signal(barrier, inc=1, device_id=parent(move), device_id_type=MESH)
 
-    for e in range(1, K + 1):
-        acc[e] = jnp.zeros(acc.shape[1:], F32)
     own_copy.wait()
     pl.semaphore_wait(barrier, peers)
 
@@ -214,6 +212,9 @@
                     @pl.when(move.here)
                     def _():
                         orbital_out(move, chunk(i), i).start()
+
+    for e in range(1, K + 1):
+        acc[e] = jnp.zeros(acc.shape[1:], F32)
 
     def forward(e, lanes, i=0):
         return pltpu.make_async_remote_copy(
@@ -427,12 +428,16 @@
         start_return(BACK_EARLY, i)
         start_return(BACK_EARLY_JOIN, i)
 
+        @pl.when(i > 1)
+        def _():
+            finish_return(BACK_EARLY, i - 2)
+
         @pl.when(i > 0)
         def _():
-            finish_return(BACK_EARLY, i - 1)
             pass_on(LATE_NEAR, i)
 
     def second_before(i):
+        at_step(i, 1, (finish_return, BACK_EARLY, 3))
         pass_on(LATE_FAR, i)
         passed_on(LATE_NEAR, i)
         passed_on(LATE_FAR, i)
@@ -443,9 +448,9 @@
         exchange(0, chunk(i), i).start()
         finish_return(BACK_EARLY_JOIN, i)
 
-        @pl.when(i > 0)
-        def _():
-            finish_return(BACK_LATE, i - 1)
+        @pl.when(i > 1)
+        def _():
+            finish_return(BACK_LATE, i - 2)
 
     table_copy.wait()
     transform([(0, 0), (0, 0)], self_update)
@@ -454,8 +459,9 @@
     pass_on(EARLY_FAR, 0)
     pass_on(EARLY_NEAR, 2)
     pair_batch(0, first_before, first_middle, first_after)
-    finish_return(BACK_EARLY, 3)
+    finish_return(BACK_EARLY, 2)
     pair_batch(1, second_before, None, second_after)
+    finish_return(BACK_LATE, 2)
     finish_return(BACK_LATE, 3)
 
     def gather(i, carry):

time: 71.7 us -> 69.5 us (0.969); the launches traced: 71.6 us -> 68.6 us
  Pallas kernels: 69.9 us -> 66.9 us
    pallas_call x1, Pallas kernels: 69.9 us -> 66.9 us  [body(): pl.pallas_call(kernel, name='exchange', out_shape=jax.ShapeDtypeStruct((1...]
where the time goes in v3:
time: 69.5 us; the launch traced here: 68.6 us
  Pallas kernels  66.9 us (96%)
  local copies, waits for them, and re-layouts  1.67 us (2%)
    pallas_call x1, Pallas kernels, body(): pl.pallas_call(kernel, name='exchange', out_shape=jax.ShapeDtypeStruct((1...  66.9 us
    unnamed x1, local copies, waits for them, and re-layouts  1.67 us

profile of v3, /device:TPU:0, one launch (start us, length us, event | category | flops | bytes accessed | tf_op | source)
XLA Modules:
  0.0 68.6 jit_solution(8796363641177060626)
XLA Ops:
  0.0 66.9 %exchange.1 = f32[16,4096]{1,0:T(8,128)} custom-call(f32[64,4096]{1,0:T(8,128)} %bitcast.2, s32[32,32]{1,0:T(8,128)} %keep_ref.1, bf16[256,256]{1,0:T(8,128)(2,1)} %constant.6.clone.wz_ref, bf16[128,128]{1,0:T(8,128)(2,1)} %constant.7.clone.wr_ref, f32[64,64,128]{2,1,0:T(8,128)} %constant.8.clone.table_hbm), custom_call_target="tpu_custom_call" | custom-call | tf_op jit(solution)/shard_map/exchange/pallas_call | solution.py:509
  66.9 1.7 %copy.7 = f32[1,16,4096]{2,1,0:T(8,128)} copy(f32[1,16,4096]{2,1,0:T(8,128)} %bitcast.3) | data formatting | bytes 524288

commit v4 on v3

--- a/solution.py
+++ b/solution.py
@@ -204,14 +204,16 @@
     def is_early(move):
         return move.e in EARLY_NEAR[move.l] or move.e in EARLY_FAR[move.l]
 
-    for early in (True, False):
-        for i in range(4):
-            for move in moves:
-                if move.slot == 0 and is_early(move) == early:
-
-                    @pl.when(move.here)
-                    def _():
-                        orbital_out(move, chunk(i), i).start()
+    def set_out(early, i):
+        for move in moves:
+            if move.slot == 0 and is_early(move) == early:
+
+                @pl.when(move.here)
+                def _():
+                    orbital_out(move, chunk(i), i).start()
+
+    for i in range(4):
+        set_out(True, i)
 
     for e in range(1, K + 1):
         acc[e] = jnp.zeros(acc.shape[1:], F32)
@@ -232,6 +234,11 @@
                         body(chip, e)
 
     def pass_on(chosen, i):
+        def relayed(chip, e):
+            return any((move.from_l, move.slot) == (chip, e + 1) for move in moves)
+
+        chosen = [sorted(chosen[chip], key=lambda e: not relayed(chip, e)) for chip in (0, 1)]
+
         def one(chip, e):
             arriving = [move for move in moves if (move.l, move.e) == (chip, e)][0]
             orbital_out(arriving, chunk(i), i).wait_recv()
@@ -296,7 +303,7 @@
             return carry
 
         lax.fori_loop(0, 64 // YC, first, 0)
-        lax.fori_loop(0, 64 // YC, second, 0)
+        lax.fori_loop(0, 64 // YC, second, 0, unroll=True)
         lax.fori_loop(0, 64 // YC, third, 0)
 
     def keep_at(i, j):
@@ -414,10 +421,13 @@
             for action, *arguments in actions:
                 action(*arguments)
 
+    def self_after(i):
+        at_step(i, 3, *[(set_out, False, k) for k in range(4)])
+        at_step(i, 2, (pass_on, EARLY_NEAR, 0))
+
     def first_before(i):
-        at_step(i, 1, (pass_on, EARLY_FAR, 1))
-        at_step(i, 2, (pass_on, EARLY_NEAR, 3), (pass_on, EARLY_FAR, 2))
-        at_step(i, 3, (pass_on, EARLY_FAR, 3))
+        for k in (1, 2, 3):
+            at_step(i, k, (pass_on, EARLY_FAR, k))
         passed_on(EARLY_NEAR, i)
         passed_on(EARLY_FAR, i)
 
@@ -453,11 +463,10 @@
             finish_return(BACK_LATE, i - 2)
 
     table_copy.wait()
-    transform([(0, 0), (0, 0)], self_update)
-    pass_on(EARLY_NEAR, 0)
-    pass_on(EARLY_NEAR, 1)
+    transform([(0, 0), (0, 0)], self_update, after=self_after)
+    for i in range(1, 4):
+        pass_on(EARLY_NEAR, i)
     pass_on(EARLY_FAR, 0)
-    pass_on(EARLY_NEAR, 2)
     pair_batch(0, first_before, first_middle, first_after)
     finish_return(BACK_EARLY, 2)
     pair_batch(1, second_before, None, second_after)

time: 69.5 us -> 67.8 us (0.976)
  Pallas kernels: 66.9 us -> 65.8 us
    pallas_call x1, Pallas kernels: 66.9 us -> 65.8 us  [body(): pl.pallas_call(kernel, name='exchange', out_shape=jax.ShapeDtypeStruct((1...]
where the time goes in v4:
time: 67.8 us; the launch traced here: 67.5 us
  Pallas kernels  65.8 us (97%)
  local copies, waits for them, and re-layouts  1.67 us (2%)
    pallas_call x1, Pallas kernels, body(): pl.pallas_call(kernel, name='exchange', out_shape=jax.ShapeDtypeStruct((1...  65.8 us
    unnamed x1, local copies, waits for them, and re-layouts  1.67 us

profile of v4, /device:TPU:0, one launch (start us, length us, event | category | flops | bytes accessed | tf_op | source)
XLA Modules:
  0.0 67.5 jit_solution(13342281157252696182)
XLA Ops:
  0.0 65.8 %exchange.1 = f32[16,4096]{1,0:T(8,128)} custom-call(f32[64,4096]{1,0:T(8,128)} %bitcast.2, s32[32,32]{1,0:T(8,128)} %keep_ref.1, bf16[256,256]{1,0:T(8,128)(2,1)} %constant.6.clone.wz_ref, bf16[128,128]{1,0:T(8,128)(2,1)} %constant.7.clone.wr_ref, f32[64,64,128]{2,1,0:T(8,128)} %constant.8.clone.table_hbm), custom_call_target="tpu_custom_call" | custom-call | tf_op jit(solution)/shard_map/exchange/pallas_call | solution.py:518
  65.8 1.7 %copy.7 = f32[1,16,4096]{2,1,0:T(8,128)} copy(f32[1,16,4096]{2,1,0:T(8,128)} %bitcast.3) | data formatting | bytes 524288

commit v5 on v4

--- a/solution.py
+++ b/solution.py
@@ -422,8 +422,9 @@
                 action(*arguments)
 
     def self_after(i):
+        at_step(i, 3, (pass_on, EARLY_NEAR, 1))
         at_step(i, 3, *[(set_out, False, k) for k in range(4)])
-        at_step(i, 2, (pass_on, EARLY_NEAR, 0))
+        at_step(i, 0, (pass_on, EARLY_NEAR, 0))
 
     def first_before(i):
         for k in (1, 2, 3):
@@ -464,7 +465,7 @@
 
     table_copy.wait()
     transform([(0, 0), (0, 0)], self_update, after=self_after)
-    for i in range(1, 4):
+    for i in range(2, 4):
         pass_on(EARLY_NEAR, i)
     pass_on(EARLY_FAR, 0)
     pair_batch(0, first_before, first_middle, first_after)

time: 67.8 us -> 67.8 us (level)
  no operation moved by 1% of the time
where the time goes in v5:
time: 67.8 us; the launch traced here: 66.8 us
  Pallas kernels  65.2 us (96%)
  local copies, waits for them, and re-layouts  1.67 us (2%)
    pallas_call x1, Pallas kernels, body(): pl.pallas_call(kernel, name='exchange', out_shape=jax.ShapeDtypeStruct((1...  65.2 us
    unnamed x1, local copies, waits for them, and re-layouts  1.67 us

profile of v5, /device:TPU:0, one launch (start us, length us, event | category | flops | bytes accessed | tf_op | source)
XLA Modules:
  0.0 66.8 jit_solution(9088196978994933849)
XLA Ops:
  0.0 65.2 %exchange.1 = f32[16,4096]{1,0:T(8,128)} custom-call(f32[64,4096]{1,0:T(8,128)} %bitcast.2, s32[32,32]{1,0:T(8,128)} %keep_ref.1, bf16[256,256]{1,0:T(8,128)(2,1)} %constant.6.clone.wz_ref, bf16[128,128]{1,0:T(8,128)(2,1)} %constant.7.clone.wr_ref, f32[64,64,128]{2,1,0:T(8,128)} %constant.8.clone.table_hbm), custom_call_target="tpu_custom_call" | custom-call | tf_op jit(solution)/shard_map/exchange/pallas_call | solution.py:519
  65.2 1.7 %copy.7 = f32[1,16,4096]{2,1,0:T(8,128)} copy(f32[1,16,4096]{2,1,0:T(8,128)} %bitcast.3) | data formatting | bytes 524288

commit v6 on v5

--- a/solution.py
+++ b/solution.py
@@ -459,9 +459,9 @@
         exchange(0, chunk(i), i).start()
         finish_return(BACK_EARLY_JOIN, i)
 
-        @pl.when(i > 1)
-        def _():
-            finish_return(BACK_LATE, i - 2)
+        @pl.when(i > 0)
+        def _():
+            finish_return(BACK_LATE, i - 1)
 
     table_copy.wait()
     transform([(0, 0), (0, 0)], self_update, after=self_after)
@@ -471,7 +471,6 @@
     pair_batch(0, first_before, first_middle, first_after)
     finish_return(BACK_EARLY, 2)
     pair_batch(1, second_before, None, second_after)
-    finish_return(BACK_LATE, 2)
     finish_return(BACK_LATE, 3)
 
     def gather(i, carry):

time: 67.8 us -> 67.8 us (level)
  no operation moved by 1% of the time
where the time goes in v6:
time: 67.8 us; the launch traced here: 66.8 us
  Pallas kernels  65.2 us (96%)
  local copies, waits for them, and re-layouts  1.67 us (2%)
    pallas_call x1, Pallas kernels, body(): pl.pallas_call(kernel, name='exchange', out_shape=jax.ShapeDtypeStruct((1...  65.2 us
    unnamed x1, local copies, waits for them, and re-layouts  1.67 us

profile of v6, /device:TPU:0, one launch (start us, length us, event | category | flops | bytes accessed | tf_op | source)
XLA Modules:
  0.0 66.8 jit_solution(6588060389790179597)
XLA Ops:
  0.0 65.2 %exchange.1 = f32[16,4096]{1,0:T(8,128)} custom-call(f32[64,4096]{1,0:T(8,128)} %bitcast.2, s32[32,32]{1,0:T(8,128)} %keep_ref.1, bf16[256,256]{1,0:T(8,128)(2,1)} %constant.6.clone.wz_ref, bf16[128,128]{1,0:T(8,128)(2,1)} %constant.7.clone.wr_ref, f32[64,64,128]{2,1,0:T(8,128)} %constant.8.clone.table_hbm), custom_call_target="tpu_custom_call" | custom-call | tf_op jit(solution)/shard_map/exchange/pallas_call | solution.py:518
  65.2 1.7 %copy.7 = f32[1,16,4096]{2,1,0:T(8,128)} copy(f32[1,16,4096]{2,1,0:T(8,128)} %bitcast.3) | data formatting | bytes 524288
